TPU v7x, 256 devices: a whole 4x4x8 slice. The times are simulated.
256 devices in a mesh: rows: 16 (over z_lo, x, core), rep: 16 (over y, z_hi).
Axes of the slice: x: 4, y: 4, z: 8 (z_hi: 4, z_lo: 2; z = z_hi * 2 + z_lo), core: 2. Of those that a mesh axis runs over, the one named last changes fastest.
Arguments:
- node_features: bfloat16 [32768, 256], P(('rows', 'rep')), may hold values from -6 to 6
- adjacency: bfloat16 [256, 64, 128, 128], P('rows', 'rep'), may hold values from -0.078125 to 0.078125
- column_ids: int32 [256, 64], P('rows', 'rep'), may hold values from 0 to 15
- block_counts: int32 [256, 16], P('rows', 'rep'), may hold values from 1 to 4, 40 in all within a row
- weight_first: bfloat16 [256, 512], replicated, may hold values from -0.375 to 0.375
- weight_second: bfloat16 [512, 256], replicated, may hold values from -0.25 to 0.25
- cotangent: bfloat16 [32768, 256], P(('rows', 'rep')), may hold values from -6 to 6
Outputs:
- embedding: bfloat16 [32768, 256], P(('rows', 'rep'))
- grad_first: float32 [256, 512], replicated
- grad_second: float32 [512, 256], replicated
Inputs may be any that keep to these rules, and one draw needn't show every extreme that they name: `block_counts`: each row block has 40 live slots over its 16 groups; some group of some row block has all 4 live.
All inputs are finite; a program needn't handle non-finite values.
Results may differ from a plain program's by a relative error of at most 0.024.
Values may be sent and summed in bfloat16 or wider, within the bound.
A program may use at most 64 MiB of HBM per device.

v0:
```python
import math
import jax
import jax.numpy as jnp
from jax import lax
from jax.sharding import PartitionSpec as P

BS = 128


def slot_weights(adjacency, block_counts, slot):
    weights = adjacency[:, slot]
    live_rows = slot < block_counts[:, 0]
    return jnp.where(live_rows[:, None, None], weights, jnp.zeros_like(weights))


def aggregate(node_field, adjacency, column_ids, block_counts):
    feature_width = node_field.shape[1]
    gathered = lax.all_gather(node_field, "rows", axis=0, tiled=True)
    blocks_in = gathered.reshape(-1, BS, feature_width)
    row_blocks = column_ids.shape[0]
    partial_sum = jnp.zeros((row_blocks, BS, feature_width), jnp.float32)
    for slot in range(column_ids.shape[1]):
        weights = slot_weights(adjacency, block_counts, slot)
        picked = blocks_in[column_ids[:, slot]]
        partial_sum = partial_sum + jnp.einsum(
            "rij,rjf->rif", weights, picked, preferred_element_type=jnp.float32
        )
    return lax.psum_scatter(
        partial_sum.reshape(row_blocks * BS, feature_width).astype(jnp.bfloat16),
        "rep",
        scatter_dimension=0,
        tiled=True,
    ).astype(jnp.float32)


def transpose_aggregate(cotangent, adjacency, column_ids, block_counts):
    feature_width = cotangent.shape[1]
    row_blocks = column_ids.shape[0]
    gathered = lax.all_gather(cotangent, "rep", axis=0, tiled=True).reshape(
        row_blocks, BS, feature_width
    )
    col_blocks = lax.axis_size("rows") * (cotangent.shape[0] // BS)
    summed = jnp.zeros((col_blocks, BS, feature_width), jnp.float32)
    for slot in range(column_ids.shape[1]):
        weights = slot_weights(adjacency, block_counts, slot)
        terms = jnp.einsum("rij,rif->rjf", weights, gathered, preferred_element_type=jnp.float32)
        summed = summed.at[column_ids[:, slot]].add(terms)
    return lax.psum_scatter(
        summed.reshape(col_blocks * BS, feature_width).astype(jnp.bfloat16),
        "rows",
        scatter_dimension=0,
        tiled=True,
    ).astype(jnp.float32)


def shards(
    node_features, adjacency, column_ids, block_counts, weight_first, weight_second, cotangent
):
    contract = (((0,), (0,)), ((), ()))
    mixed_input = aggregate(node_features, adjacency, column_ids, block_counts).astype(jnp.bfloat16)
    pre_first = jnp.dot(mixed_input, weight_first, preferred_element_type=jnp.float32)
    hidden = jax.nn.silu(pre_first).astype(jnp.bfloat16)
    second_in = jnp.dot(hidden, weight_second, preferred_element_type=jnp.float32).astype(
        jnp.bfloat16
    )
    embedding = aggregate(second_in, adjacency, column_ids, block_counts).astype(jnp.bfloat16)
    upstream = transpose_aggregate(cotangent, adjacency, column_ids, block_counts).astype(
        jnp.bfloat16
    )
    node_total = node_features.shape[0] * lax.axis_size("rows") * lax.axis_size("rep")
    scale_factor = 1.0 / math.sqrt(node_total)
    local_second = lax.dot_general(hidden, upstream, contract, preferred_element_type=jnp.float32)
    back_hidden = lax.dot_general(
        upstream, weight_second, (((1,), (1,)), ((), ())), preferred_element_type=jnp.float32
    )
    sigmoid_gate = jax.nn.sigmoid(pre_first)
    back_pre = (back_hidden * sigmoid_gate * (1.0 + pre_first * (1.0 - sigmoid_gate))).astype(
        jnp.bfloat16
    )
    local_first = lax.dot_general(
        mixed_input, back_pre, contract, preferred_element_type=jnp.float32
    )
    grad_first, grad_second = lax.psum((local_first, local_second), ("rows", "rep"))
    return (embedding, grad_first * scale_factor, grad_second * scale_factor)


def solution(mesh):
    in_specs = (
        P(("rows", "rep"), None),
        P("rows", "rep", None, None),
        P("rows", "rep"),
        P("rows", "rep"),
        P(),
        P(),
        P(("rows", "rep"), None),
    )
    out_specs = (P(("rows", "rep"), None), P(), P())
    return jax.shard_map(shards, mesh=mesh, in_specs=in_specs, out_specs=out_specs, check_vma=False)
```

profile of v0, /device:TPU:2, one launch (start us, length us, event | category | flops | bytes accessed | tf_op | source)
XLA Modules:
  0.0 649.3 jit_solution(16340234801673374021)
XLA Ops:
  10.2 37.3 %all-gather.4.cloned.1.call-done = bf16[2048,256]{1,0:T(8,128)(2,1)} async-done(((bf16[128,256]{1,0:T(8,128)(2,1)}), bf16[2048,256]{1,0:T(8,128)(2,1)}) %all-gather.4.cloned.1.call-update) | async-done | bytes 1048592 | tf_op jit(solution)/shard_map/all_gather | solution.py:18
  47.6 2.9 gather_fusion.2
  50.5 1.6 gather_fusion
  52.1 1.6 gather_fusion.1
  53.7 1.6 gather_fusion.3
  55.3 1.8 fusion.21
  60.6 43.4 %all-gather.8.cloned.1.call-done = bf16[2048,256]{1,0:T(8,128)(2,1)} async-done(((bf16[128,256]{1,0:T(8,128)(2,1)}), bf16[2048,256]{1,0:T(8,128)(2,1)}) %all-gather.8.cloned.1.call-update) | async-done | bytes 1048592 | tf_op jit(solution)/shard_map/all_gather | solution.py:39
  104.0 3.3 fusion.16
  107.5 3.5 scatter_fusion
  111.1 3.1 fusion.13
  114.2 3.5 scatter_fusion.1
  117.7 3.1 fusion.19
  120.8 3.5 scatter_fusion.2
  124.4 3.1 fusion.22
  127.5 3.5 scatter_fusion.3
  132.2 58.8 %reduce-scatter.4.cloned.1.call-done = bf16[128,256]{1,0:T(8,128)(2,1)} async-done(((bf16[2048,256]{1,0:T(8,128)(2,1)}), bf16[128,256]{1,0:T(8,128)(2,1)}) %reduce-scatter.4.cloned.1.call-update) | async-done | bytes 65552 | tf_op jit(solution)/shard_map/reduce_scatter | solution.py:28
  193.1 58.3 %reduce-scatter.8.cloned.1.call-done = bf16[128,256]{1,0:T(8,128)(2,1)} async-done(((bf16[2048,256]{1,0:T(8,128)(2,1)}), bf16[128,256]{1,0:T(8,128)(2,1)}) %reduce-scatter.8.cloned.1.call-update) | async-done | bytes 65552 | tf_op jit(solution)/shard_map/reduce_scatter | solution.py:48
  251.4 1.9 fusion.12
  253.3 2.1 fusion.2
  255.5 34.7 %all-gather.6.cloned.1.call-done = bf16[2048,256]{1,0:T(8,128)(2,1)} async-done(((bf16[128,256]{1,0:T(8,128)(2,1)}), bf16[2048,256]{1,0:T(8,128)(2,1)}) %all-gather.6.cloned.1.call-update) | async-done | bytes 1048592 | tf_op jit(solution)/shard_map/all_gather | solution.py:18
  290.2 2.9 gather_fusion.6
  293.1 1.6 gather_fusion.4
  294.7 1.6 gather_fusion.5
  296.3 3.1 fusion.20
  299.4 1.8 fusion.17
  301.3 1.8 fusion.14
  303.1 1.7 gather_fusion.7
  304.8 4.8 add_convert_fusion
  309.5 243.3 %all-reduce.3.cloned.1.call-done = (f32[256,512]{1,0:T(8,128)}, f32[512,256]{1,0:T(8,128)}) async-done(((f32[256,512]{1,0:T(8,128)}, f32[512,256]{1,0:T(8,128)}), (f32[256,512]{1,0:T(8,128)}, f32[512,256]{1,0:T(8,128)})) %all-reduce.3.cloned.1.call-update) | async-done | bytes 1048592 | tf_op jit(solution)/shard_map/psum | solution.py:83
  552.9 1.9 broadcast_multiply_fusion.1
  554.7 1.9 broadcast_multiply_fusion
  556.6 85.8 %reduce-scatter.6.cloned.1.call-done = bf16[128,256]{1,0:T(8,128)(2,1)} async-done(((bf16[2048,256]{1,0:T(8,128)(2,1)}), bf16[128,256]{1,0:T(8,128)(2,1)}) %reduce-scatter.6.cloned.1.call-update) | async-done | bytes 65552 | tf_op jit(solution)/shard_map/reduce_scatter | solution.py:28
  (51 shorter events, 9.9 us)
Async XLA Ops:
  7.2 185.0 %copy-start = (bf16[512,256]{1,0:T(8,128)(2,1)S(1)}, bf16[512,256]{1,0:T(8,128)(2,1)}, u32[]{:S(2)}) copy-start(bf16[512,256]{1,0:T(8,128)(2,1)} %param.12) | copy-start | bytes 786436
  7.2 40.4 %all-gather.4.cloned.1.call-start = ((), (), s32[]{:S(2)}) async-start(), calls=%async_computation.3 | async-start | bytes 1114112 | tf_op jit(solution)/shard_map/all_gather | solution.py:18
  7.9 96.1 %all-gather.8.cloned.1.call-start = ((), (), s32[]{:S(2)}) async-start(), calls=%async_computation.7 | async-start | bytes 1114112 | tf_op jit(solution)/shard_map/all_gather | solution.py:39
  8.7 182.4 %reduce-scatter.4.cloned.1.call-start = ((), (), s32[]{:S(2)}) async-start(), calls=%async_computation.4 | async-start | bytes 1114112 | tf_op jit(solution)/shard_map/reduce_scatter | solution.py:28
  47.6 2.9 copy-start.4
  52.1 3.2 copy-start.1
  55.3 1.8 copy-start.8
  57.1 1.2 copy-start.9
  57.6 1.3 copy-start.6
  60.5 190.9 %reduce-scatter.8.cloned.1.call-start = ((), (), s32[]{:S(2)}) async-start(), calls=%async_computation.8 | async-start | bytes 1114112 | tf_op jit(solution)/shard_map/reduce_scatter | solution.py:48
  107.5 3.5 copy-start.5
  131.0 60.1 %copy-start.11 = (bf16[256,512]{1,0:T(8,128)(2,1)S(1)}, bf16[256,512]{1,0:T(8,128)(2,1)}, u32[]{:S(2)}) copy-start(bf16[256,512]{1,0:T(8,128)(2,1)} %param.11) | copy-start | bytes 786436
  132.2 158.0 %all-gather.6.cloned.1.call-start = ((), (), s32[]{:S(2)}) async-start(), calls=%async_computation.5 | async-start | bytes 1114112 | tf_op jit(solution)/shard_map/all_gather | solution.py:18
  191.1 62.3 %copy-start.12 = (bf16[128,256]{1,0:T(8,128)(2,1)S(1)}, bf16[128,256]{1,0:T(8,128)(2,1)}, u32[]{:S(2)}) copy-start(bf16[128,256]{1,0:T(8,128)(2,1)} %reduce-scatter.4.cloned.1.call-done) | copy-start | bytes 196612
  193.0 359.8 %all-reduce.3.cloned.1.call-start = ((), (), s32[]{:S(2)}) async-start(), calls=%async_computation.9 | async-start | bytes 2097152 | tf_op jit(solution)/shard_map/psum | solution.py:83
  255.4 387.0 %reduce-scatter.6.cloned.1.call-start = ((), (), s32[]{:S(2)}) async-start(), calls=%async_computation.6 | async-start | bytes 1114112 | tf_op jit(solution)/shard_map/reduce_scatter | solution.py:28
  290.2 2.9 copy-start.3
  293.1 3.2 copy-start.2
  296.3 3.1 copy-start.10
  299.4 1.8 copy-start.7
Sparse Core Ops, SparseCore 0:
  9.9 37.6 all-gather.3
  50.0 53.9 all-gather.7
  107.5 83.4 reduce-scatter.3
  193.6 57.7 reduce-scatter.7
  253.7 36.4 all-gather.5
  296.2 256.5 all-reduce.2
  557.3 85.0 reduce-scatter.5
where the time goes:
time: 650 us; the launch traced here: 649 us
  waiting for transfers between devices  563 us (87%)
  matrix products  34.5 us (5%)
  other arithmetic  20.4 us (3%)
  local copies, waits for them, and re-layouts  16.5 us (3%)
  between operations  14.3 us (2%)
    psum x1, waiting for transfers between devices, shards(): lax.psum((local_first, local_second), ('rows', 'rep'))  243 us
    reduce_scatter x2, waiting for transfers between devices, aggregate(): lax.psum_scatter(partial_sum.reshape(row_blocks * BS, feature_width).asty...  145 us
    all_gather x2, waiting for transfers between devices, aggregate(): gathered = lax.all_gather(node_field, 'rows', axis=0, tiled=True)  72.1 us
    reduce_scatter x1, waiting for transfers between devices, transpose_aggregate(): lax.psum_scatter(summed.reshape(col_blocks * BS, feature_width).astype(jn...  58.3 us
    all_gather x1, waiting for transfers between devices, transpose_aggregate(): lax.all_gather(cotangent, 'rep', axis=0, tiled=True)  43.4 us
    dot_general x8, matrix products, aggregate(): jnp.einsum('rij,rjf->rif', weights, picked, preferred_element_type=jnp.fl...  15.9 us
    gather x8, local copies, waits for them, and re-layouts, aggregate(): picked = blocks_in[column_ids[:, slot]]  15.5 us
    scatter-add x4, other arithmetic, transpose_aggregate(): summed = summed.at[column_ids[:, slot]].add(terms)  14.1 us
  transfers between devices with their start and end apart: 7, of which 7 were waited for; matrix products, arithmetic and copies ran while one was open for 11% of the time, Pallas kernels for 0%

commit v1 on v0

--- a/solution.py
+++ b/solution.py
@@ -5,6 +5,11 @@
 from jax.sharding import PartitionSpec as P
 
 BS = 128
+
+
+def by_each_axis(array, inner_axis, outer_axis):
+    partial = lax.psum(array, inner_axis)
+    return lax.psum(partial, outer_axis)
 
 
 def slot_weights(adjacency, block_counts, slot):
@@ -80,7 +85,7 @@
     local_first = lax.dot_general(
         mixed_input, back_pre, contract, preferred_element_type=jnp.float32
     )
-    grad_first, grad_second = lax.psum((local_first, local_second), ("rows", "rep"))
+    grad_first, grad_second = by_each_axis((local_first, local_second), "rows", "rep")
     return (embedding, grad_first * scale_factor, grad_second * scale_factor)
 
 

time: 650 us -> 689 us (1.060)
  waiting for transfers between devices: 563 us -> 608 us
  matrix products: 34.5 us -> 27.2 us
    psum x1 -> x2, waiting for transfers between devices: 243 us -> 282 us  [the longest x1 160 us: by_each_axis(): return lax.psum(partial, outer_axis)]
    dot_general x8, matrix products: 15.9 us -> 8.63 us  [aggregate(): jnp.einsum('rij,rjf->rif', weights, picked, preferred_element_type=jnp.fl...]
  transfers between devices with their start and end apart: 7 -> 8, of which waited for: 7 -> 8; matrix products, arithmetic and copies ran while one was open for 11% -> 9% of each run, Pallas kernels for 0% -> 0%
where the time goes in v1:
time: 689 us; the launch traced here: 688 us
  waiting for transfers between devices  608 us (88%)
  matrix products  27.2 us (4%)
  other arithmetic  20.4 us (3%)
  local copies, waits for them, and re-layouts  17.9 us (3%)
  between operations  14.3 us (2%)
    psum x1, waiting for transfers between devices, by_each_axis(): return lax.psum(partial, outer_axis)  160 us
    reduce_scatter x2, waiting for transfers between devices, aggregate(): lax.psum_scatter(partial_sum.reshape(row_blocks * BS, feature_width).asty...  143 us
    psum x1, waiting for transfers between devices, by_each_axis(): partial = lax.psum(array, inner_axis)  122 us
    all_gather x2, waiting for transfers between devices, aggregate(): gathered = lax.all_gather(node_field, 'rows', axis=0, tiled=True)  78.9 us
    reduce_scatter x1, waiting for transfers between devices, transpose_aggregate(): lax.psum_scatter(summed.reshape(col_blocks * BS, feature_width).astype(jn...  59.3 us
    all_gather x1, waiting for transfers between devices, transpose_aggregate(): lax.all_gather(cotangent, 'rep', axis=0, tiled=True)  43.5 us
    gather x8, local copies, waits for them, and re-layouts, aggregate(): picked = blocks_in[column_ids[:, slot]]  15.4 us
    scatter-add x4, other arithmetic, transpose_aggregate(): summed = summed.at[column_ids[:, slot]].add(terms)  14.1 us
  transfers between devices with their start and end apart: 8, of which 8 were waited for; matrix products, arithmetic and copies ran while one was open for 9% of the time, Pallas kernels for 0%

profile of v1, /device:TPU:2, one launch (start us, length us, event | category | flops | bytes accessed | tf_op | source)
XLA Modules:
  0.0 688.2 jit_solution(655920282865687233)
XLA Ops:
  10.2 37.3 %all-gather.4.cloned.1.call-done = bf16[2048,256]{1,0:T(8,128)(2,1)} async-done(((bf16[128,256]{1,0:T(8,128)(2,1)}), bf16[2048,256]{1,0:T(8,128)(2,1)}) %all-gather.4.cloned.1.call-update) | async-done | bytes 1048592 | tf_op jit(solution)/shard_map/all_gather | solution.py:23
  47.6 2.9 gather_fusion.2
  50.5 1.6 gather_fusion
  52.1 1.6 gather_fusion.1
  53.7 1.6 gather_fusion.3
  55.3 1.8 fusion.21
  58.9 1.6 add_convert_fusion.1
  60.5 43.5 %all-gather.8.cloned.1.call-done = bf16[2048,256]{1,0:T(8,128)(2,1)} async-done(((bf16[128,256]{1,0:T(8,128)(2,1)}), bf16[2048,256]{1,0:T(8,128)(2,1)}) %all-gather.8.cloned.1.call-update) | async-done | bytes 1048592 | tf_op jit(solution)/shard_map/all_gather | solution.py:44
  104.0 3.3 fusion.16
  107.5 3.5 scatter_fusion
  111.1 3.1 fusion.13
  114.2 3.5 scatter_fusion.1
  117.7 3.1 fusion.19
  120.9 3.5 scatter_fusion.2
  124.4 3.1 fusion.22
  127.5 3.5 scatter_fusion.3
  132.2 58.9 %reduce-scatter.4.cloned.1.call-done = bf16[128,256]{1,0:T(8,128)(2,1)} async-done(((bf16[2048,256]{1,0:T(8,128)(2,1)}), bf16[128,256]{1,0:T(8,128)(2,1)}) %reduce-scatter.4.cloned.1.call-update) | async-done | bytes 65552 | tf_op jit(solution)/shard_map/reduce_scatter | solution.py:33
  192.1 59.3 %reduce-scatter.8.cloned.1.call-done = bf16[128,256]{1,0:T(8,128)(2,1)} async-done(((bf16[2048,256]{1,0:T(8,128)(2,1)}), bf16[128,256]{1,0:T(8,128)(2,1)}) %reduce-scatter.8.cloned.1.call-update) | async-done | bytes 65552 | tf_op jit(solution)/shard_map/reduce_scatter | solution.py:53
  251.5 1.9 fusion.12
  253.4 2.1 fusion.2
  256.5 122.0 %all-reduce.7.cloned.1.call-done = (f32[256,512]{1,0:T(8,128)}, f32[512,256]{1,0:T(8,128)}) async-done(((f32[256,512]{1,0:T(8,128)}, f32[512,256]{1,0:T(8,128)}), (f32[256,512]{1,0:T(8,128)}, f32[512,256]{1,0:T(8,128)})) %all-reduce.7.cloned.1.call-update) | async-done | bytes 1048592 | tf_op jit(solution)/shard_map/psum | solution.py:11
  378.6 41.5 %all-gather.6.cloned.1.call-done = bf16[2048,256]{1,0:T(8,128)(2,1)} async-done(((bf16[128,256]{1,0:T(8,128)(2,1)}), bf16[2048,256]{1,0:T(8,128)(2,1)}) %all-gather.6.cloned.1.call-update) | async-done | bytes 1048592 | tf_op jit(solution)/shard_map/all_gather | solution.py:23
  420.1 2.9 gather_fusion.6
  423.0 1.6 gather_fusion.4
  424.6 1.6 gather_fusion.5
  426.2 1.6 gather_fusion.7
  427.8 1.8 fusion.20
  432.1 1.6 add_convert_fusion
  433.6 160.1 %all-reduce.5.cloned.1.call-done = (f32[256,512]{1,0:T(8,128)}, f32[512,256]{1,0:T(8,128)}) async-done(((f32[256,512]{1,0:T(8,128)}, f32[512,256]{1,0:T(8,128)}), (f32[256,512]{1,0:T(8,128)}, f32[512,256]{1,0:T(8,128)})) %all-reduce.5.cloned.1.call-update) | async-done | bytes 1048592 | tf_op jit(solution)/shard_map/psum | solution.py:12
  593.8 1.9 broadcast_multiply_fusion.1
  595.6 1.9 broadcast_multiply_fusion
  597.5 83.9 %reduce-scatter.6.cloned.1.call-done = bf16[128,256]{1,0:T(8,128)(2,1)} async-done(((bf16[2048,256]{1,0:T(8,128)(2,1)}), bf16[128,256]{1,0:T(8,128)(2,1)}) %reduce-scatter.6.cloned.1.call-update) | async-done | bytes 65552 | tf_op jit(solution)/shard_map/reduce_scatter | solution.py:33
  (54 shorter events, 10.7 us)
Async XLA Ops:
  7.2 246.2 %copy-start = (bf16[512,256]{1,0:T(8,128)(2,1)S(1)}, bf16[512,256]{1,0:T(8,128)(2,1)}, u32[]{:S(2)}) copy-start(bf16[512,256]{1,0:T(8,128)(2,1)} %param.12) | copy-start | bytes 786436
  7.2 40.4 %all-gather.4.cloned.1.call-start = ((), (), s32[]{:S(2)}) async-start(), calls=%async_computation.3 | async-start | bytes 1114112 | tf_op jit(solution)/shard_map/all_gather | solution.py:23
  7.9 96.1 %all-gather.8.cloned.1.call-start = ((), (), s32[]{:S(2)}) async-start(), calls=%async_computation.7 | async-start | bytes 1114112 | tf_op jit(solution)/shard_map/all_gather | solution.py:44
  8.7 182.4 %reduce-scatter.4.cloned.1.call-start = ((), (), s32[]{:S(2)}) async-start(), calls=%async_computation.4 | async-start | bytes 1114112 | tf_op jit(solution)/shard_map/reduce_scatter | solution.py:33
  47.6 2.9 copy-start.3
  52.1 3.2 copy-start.1
  55.3 1.8 copy-start.10
  57.1 1.2 copy-start.11
  57.6 1.3 copy-start.7
  60.5 191.0 %reduce-scatter.8.cloned.1.call-start = ((), (), s32[]{:S(2)}) async-start(), calls=%async_computation.8 | async-start | bytes 1114112 | tf_op jit(solution)/shard_map/reduce_scatter | solution.py:53
  107.5 3.5 copy-start.5
  131.0 60.1 %copy-start.12 = (bf16[256,512]{1,0:T(8,128)(2,1)S(1)}, bf16[256,512]{1,0:T(8,128)(2,1)}, u32[]{:S(2)}) copy-start(bf16[256,512]{1,0:T(8,128)(2,1)} %param.11) | copy-start | bytes 786436
  132.2 246.3 %all-reduce.7.cloned.1.call-start = ((), (), s32[]{:S(2)}) async-start(), calls=%async_computation.10 | async-start | bytes 2097152 | tf_op jit(solution)/shard_map/psum | solution.py:11
  255.5 164.6 %all-gather.6.cloned.1.call-start = ((), (), s32[]{:S(2)}) async-start(), calls=%async_computation.5 | async-start | bytes 1114112 | tf_op jit(solution)/shard_map/all_gather | solution.py:23
  256.4 337.3 %all-reduce.5.cloned.1.call-start = ((), (), s32[]{:S(2)}) async-start(), calls=%async_computation.9 | async-start | bytes 2097152 | tf_op jit(solution)/shard_map/psum | solution.py:12
  378.5 302.9 %reduce-scatter.6.cloned.1.call-start = ((), (), s32[]{:S(2)}) async-start(), calls=%async_computation.6 | async-start | bytes 1114112 | tf_op jit(solution)/shard_map/reduce_scatter | solution.py:33
  420.1 2.9 copy-start.4
  424.6 3.2 copy-start.2
  427.8 1.8 copy-start.9
  429.6 1.2 copy-start.8
  430.8 1.2 copy-start.6
Sparse Core Ops, SparseCore 0:
  9.9 37.6 all-gather.3
  50.0 53.9 all-gather.7
  107.5 83.5 reduce-scatter.3
  193.6 57.7 reduce-scatter.7
  255.6 122.8 all-reduce.6
  380.9 39.1 all-gather.5
  422.9 170.7 all-reduce.4
  597.8 83.5 reduce-scatter.5
